TPU v7x, 32 devices: a whole 2x2x4 slice. The times are simulated.
32 devices in a mesh: groups: 2 (over x), shard: 16 (over z, y, core).
Axes of the slice: x: 2, y: 2, z: 4, core: 2. Of those that a mesh axis runs over, the one named last changes fastest.
Arguments:
- embeddings: float32 [8192, 1024], P(('groups', 'shard')), parts along dimension 0, as said below
- dest_owner: int32 [8192], P(('groups', 'shard')), parts along dimension 0, may hold values from 0 to 15, as said below
- member_cluster: int32 [8192], P(('groups', 'shard')), parts along dimension 0, may hold values from 0 to 31
- order: int32 [8192], P(('groups', 'shard')), parts along dimension 0, may hold values from 0 to 4095, each once
Outputs:
- max_similarity: float32 [8192], P(('groups', 'shard')), parts along dimension 0
- centroids: float32 [1024, 1024], P(('groups', 'shard')), parts along dimension 0
There are 2 independent parts, one for each index of `groups`. A program takes and returns all parts, laid end to end along the dimension named above; each array names one. Nothing has to cross between parts.
Inputs may be any that keep to these rules, and one draw needn't show every extreme that they name: `dest_owner`: the rows of one device name any one owner at most 32 times; one owner, the same for all devices of a part, is named exactly 32 times by every device. `order`: each document has its own rank. `embeddings`: rows have norms of widely different sizes.
All inputs are finite; a program needn't handle non-finite values.
Results may differ from a plain program's by a relative error of at most 0.0017.
Values may be sent and summed in bfloat16 or wider, within the bound.
A program may use at most 64 MiB of HBM per device.

v0:
```python
import jax
import jax.numpy as jnp
from jax import lax
from jax.sharding import PartitionSpec as P

CL_DEV = 32


EPSILON = 1e-06


def per_device(embeddings, dest_owner, member_cluster, order):
    owners = lax.axis_size("shard")
    rows_here = embeddings.shape[0]
    features = embeddings.shape[1]
    capacity = 2 * rows_here // owners
    slots = owners * capacity
    squares = jnp.sum(embeddings * embeddings, axis=1, keepdims=True)
    unit_rows = (embeddings * lax.rsqrt(squares + EPSILON)).astype(jnp.bfloat16)
    owner_table = (dest_owner[:, None] == jnp.arange(owners, dtype=jnp.int32)[None, :]).astype(
        jnp.float32
    )
    positions = jnp.arange(rows_here, dtype=jnp.int32)
    before = (positions[:, None] > positions[None, :]).astype(jnp.float32)
    earlier = jnp.dot(before, owner_table, precision=lax.Precision.HIGHEST)
    rank = jnp.sum(earlier * owner_table, axis=1).astype(jnp.int32)
    slot_index = dest_owner * capacity + rank
    send_rows = jnp.zeros((slots, features), jnp.bfloat16).at[slot_index].set(unit_rows)
    send_cluster = jnp.full((slots,), -1, jnp.int32).at[slot_index].set(member_cluster)
    send_order = jnp.zeros((slots,), jnp.int32).at[slot_index].set(order)
    recv_rows, recv_cluster, recv_order = (
        lax.all_to_all(send_rows, "shard", split_axis=0, concat_axis=0, tiled=True),
        lax.all_to_all(send_cluster, "shard", split_axis=0, concat_axis=0, tiled=True),
        lax.all_to_all(send_order, "shard", split_axis=0, concat_axis=0, tiled=True),
    )
    block = min(512, slots)

    def block_max(start):
        scores = lax.dot_general(
            recv_rows, recv_rows, (((1,), (1,)), ((), ())), preferred_element_type=jnp.float32
        )
        allowed = (recv_cluster[:, None] == recv_cluster[None, :]) & (recv_cluster[None, :] >= 0)
        allowed = allowed & (recv_order[None, :] < recv_order[:, None])
        return jnp.max(jnp.where(allowed, scores, jnp.float32(-1.0)), axis=1)

    block_starts = jnp.arange(slots // block, dtype=jnp.int32) * block
    maxima = lax.map(block_max, block_starts).reshape(slots)
    returned = lax.all_to_all(maxima, "shard", split_axis=0, concat_axis=0, tiled=True)
    max_similarity = returned[slot_index]
    global_cluster = dest_owner * CL_DEV + member_cluster
    wanted = jnp.arange(CL_DEV * lax.axis_size("shard"), dtype=jnp.int32)
    member_table = (wanted[:, None] == global_cluster[None, :]).astype(jnp.bfloat16)
    sums = lax.psum_scatter(
        jnp.dot(member_table, unit_rows, preferred_element_type=jnp.float32),
        "shard",
        scatter_dimension=0,
        tiled=True,
    )
    centroids = sums * lax.rsqrt(jnp.mean(sums * sums, axis=1, keepdims=True) + EPSILON)
    return (max_similarity, centroids)


def solution(mesh):
    in_specs = (
        P(("groups", "shard"), None),
        P(("groups", "shard")),
        P(("groups", "shard")),
        P(("groups", "shard")),
    )
    out_specs = (P(("groups", "shard")), P(("groups", "shard"), None))
    return jax.shard_map(
        per_device, mesh=mesh, in_specs=in_specs, out_specs=out_specs, check_vma=False
    )
```

profile of v0, /device:TPU:0, one launch (start us, length us, event | category | flops | bytes accessed | tf_op | source)
XLA Modules:
  0.0 102.4 jit_solution(17011886751437384698)
XLA Ops:
  7.2 0.0 reduce-scatter.2.cloned.1.call-start
  7.2 1.0 fusion.1
  8.2 1.4 %multiply_reduce_fusion = f32[256]{0:T(256)S(1)} fusion(f32[256,1024]{1,0:T(8,128)} %param.4), kind=kLoop, calls=%fused_computation.9 | loop fusion | flops 524032 | bytes 1049600 | tf_op jit(solution)/shard_map/reduce_sum | solution.py:18
  9.5 0.7 multiply_add_fusion
  10.3 3.2 %fusion.4 = f32[512,1024]{1,0:T(8,128)} fusion(s32[256]{0:T(256)S(1)} %get-tuple-element.12, f32[256,1024]{1,0:T(8,128)} %param.4, f32[256]{0:T(256)S(1)} %add_rsqrt_fusion), kind=kOutput, calls=%fused_computation.13 | convolution fusion | flops 269090816 | bytes 3147776 | tf_op jit(solution)/shard_map/dot_general | solution.py:54
  13.4 0.0 reduce-scatter.2.cloned.1.call-update
  13.5 1.6 %scatter_custom_fusion.1 = s32[512]{0:T(512)S(1)} fusion(s32[256]{0:T(256)S(1)} %get-tuple-element.13, s32[256]{0:T(256)} %param.7, s32[]{:T(128)} %constant.13.clone.1), kind=kCustom, calls=%fused_computation.23 | custom fusion | bytes 2560 | tf_op jit(solution)/shard_map/scatter | solution.py:30
  15.0 0.7 all_to_all.30
  15.7 7.4 %all-to-all-start.1 = ((s32[16,32,1]{1,2,0:T(1,128)}), s32[16,32,1]{1,2,0:T(1,128)S(1)}, u32[]{:S(2)}, u32[]{:S(2)}) async-start(s32[16,32,1]{1,2,0:T(1,128)} %bitcast.1), calls=%async_computation.1 | async-start | bytes 16384 | tf_op jit(solution)/shard_map/all_to_all | solution.py:34
  23.1 1.6 %scatter_custom_fusion = s32[512]{0:T(512)S(1)} fusion(s32[256]{0:T(256)S(1)} %get-tuple-element.13, s32[256]{0:T(256)} %param.6, s32[]{:T(128)} %constant.10.clone.1), kind=kCustom, calls=%fused_computation.26 | custom fusion | bytes 2560 | tf_op jit(solution)/shard_map/scatter | solution.py:29
  24.7 0.7 all_to_all.28
  25.3 4.1 %all-to-all-done.1 = s32[16,32,1]{1,2,0:T(1,128)S(1)} async-done(((s32[16,32,1]{1,2,0:T(1,128)}), s32[16,32,1]{1,2,0:T(1,128)S(1)}, u32[]{:S(2)}, u32[]{:S(2)}) %all-to-all-start.1) | async-done | bytes 2080 | tf_op jit(solution)/shard_map/all_to_all | solution.py:34
  29.4 3.4 %all-to-all-start = ((s32[16,32,1]{1,2,0:T(1,128)}), s32[16,32,1]{1,2,0:T(1,128)S(1)}, u32[]{:S(2)}, u32[]{:S(2)}) async-start(s32[16,32,1]{1,2,0:T(1,128)} %bitcast), calls=%async_computation | async-start | bytes 16384 | tf_op jit(solution)/shard_map/all_to_all | solution.py:33
  32.9 2.7 %scatter_custom_fusion.2 = bf16[512,1024]{1,0:T(8,128)(2,1)} fusion(s32[256]{0:T(256)S(1)} %get-tuple-element.13, bf16[]{:T(256)} %constant.15.clone.1, f32[256,1024]{1,0:T(8,128)S(1)} %copy-done, f32[256]{0:T(256)S(1)} %add_rsqrt_fusion), kind=kCustom, calls=%fused_computation.11 | custom fusion | flops 524288 | bytes 2098178 | tf_op jit(solution)/shard_map/scatter | solution.py:28
  35.6 3.6 %all-to-all-done = s32[16,32,1]{1,2,0:T(1,128)S(1)} async-done(((s32[16,32,1]{1,2,0:T(1,128)}), s32[16,32,1]{1,2,0:T(1,128)S(1)}, u32[]{:S(2)}, u32[]{:S(2)}) %all-to-all-start) | async-done | bytes 2080 | tf_op jit(solution)/shard_map/all_to_all | solution.py:33
  39.2 3.7 %all-to-all-start.2 = ((bf16[16,32,1024]{2,1,0:T(8,128)(2,1)}), bf16[16,32,1024]{2,1,0:T(8,128)(2,1)S(1)}, u32[]{:S(2)}, u32[]{:S(2)}) async-start(bf16[16,32,1024]{2,1,0:T(8,128)(2,1)} %bitcast.2), calls=%async_computation.2 | async-start | bytes 2097152 | tf_op jit(solution)/shard_map/all_to_all | solution.py:32
  42.9 0.5 broadcast.65
  43.4 0.7 reduce.9
  44.1 0.1 lt.30
  44.1 0.7 reduce.10
  44.8 0.1 eq.51
  44.9 29.4 %all-to-all-done.2 = bf16[16,32,1024]{2,1,0:T(8,128)(2,1)S(1)} async-done(((bf16[16,32,1024]{2,1,0:T(8,128)(2,1)}), bf16[16,32,1024]{2,1,0:T(8,128)(2,1)S(1)}, u32[]{:S(2)}, u32[]{:S(2)}) %all-to-all-start.2) | async-done | bytes 1048608 | tf_op jit(solution)/shard_map/all_to_all | solution.py:32
  74.4 0.8 fusion
  75.2 0.7 all_to_all.35
  75.9 6.9 %all-to-all-start.3 = ((f32[16,32,1]{1,2,0:T(1,128)}), f32[16,32,1]{1,2,0:T(1,128)S(1)}, u32[]{:S(2)}, u32[]{:S(2)}) async-start(f32[16,32,1]{1,2,0:T(1,128)} %bitcast.4), calls=%async_computation.3 | async-start | bytes 16384 | tf_op jit(solution)/shard_map/all_to_all | solution.py:48
  82.8 6.3 %all-to-all-done.3 = f32[16,32,1]{1,2,0:T(1,128)S(1)} async-done(((f32[16,32,1]{1,2,0:T(1,128)}), f32[16,32,1]{1,2,0:T(1,128)S(1)}, u32[]{:S(2)}, u32[]{:S(2)}) %all-to-all-start.3) | async-done | bytes 2080 | tf_op jit(solution)/shard_map/all_to_all | solution.py:48
  89.1 0.5 broadcast.67
  89.6 0.7 reduce.11
  90.3 0.1 all_to_all.37
  90.4 2.5 %gather_fusion = f32[256]{0:T(256)} fusion(f32[512]{0:T(512)S(1)} %all_to_all.37, s32[1024]{0:T(1024)S(1)} %pad_clamp_fusion), kind=kCustom, calls=%fused_computation | custom fusion | bytes 3072 | tf_op jit(solution)/shard_map/gather | solution.py:49
  92.9 1.0 multiply_reduce_fusion.1
  93.9 1.6 %broadcast_multiply_fusion = f32[32,1024]{1,0:T(8,128)} fusion(f32[32,1024]{1,0:T(8,128)} %reduce-scatter.2.cloned.1.call-done, f32[32]{0:T(128)S(1)} %add_rsqrt_fusion.1), kind=kLoop, calls=%fused_computation.17 | loop fusion | flops 32768 | bytes 262272 | tf_op jit(solution)/shard_map/mul | solution.py:59
  (7 shorter events, 0.0 us)
Async XLA Ops:
  7.2 85.7 %reduce-scatter.2.cloned.1.call-start = ((), (), s32[]{:S(2)}) async-start(), calls=%async_computation.5 | async-start | bytes 2228224 | tf_op jit(solution)/shard_map/reduce_scatter | solution.py:53
  10.3 22.6 %copy-start = (f32[256,1024]{1,0:T(8,128)S(1)}, f32[256,1024]{1,0:T(8,128)}, u32[]{:S(2)}) copy-start(f32[256,1024]{1,0:T(8,128)} %param.4) | copy-start | bytes 3145732
  15.7 13.7 %all-to-all-start.1 = ((s32[16,32,1]{1,2,0:T(1,128)}), s32[16,32,1]{1,2,0:T(1,128)S(1)}, u32[]{:S(2)}, u32[]{:S(2)}) async-start(s32[16,32,1]{1,2,0:T(1,128)} %bitcast.1), calls=%async_computation.1 | async-start | bytes 16384 | tf_op jit(solution)/shard_map/all_to_all | solution.py:34
  29.4 9.8 %all-to-all-start = ((s32[16,32,1]{1,2,0:T(1,128)}), s32[16,32,1]{1,2,0:T(1,128)S(1)}, u32[]{:S(2)}, u32[]{:S(2)}) async-start(s32[16,32,1]{1,2,0:T(1,128)} %bitcast), calls=%async_computation | async-start | bytes 16384 | tf_op jit(solution)/shard_map/all_to_all | solution.py:33
  39.2 35.1 %all-to-all-start.2 = ((bf16[16,32,1024]{2,1,0:T(8,128)(2,1)}), bf16[16,32,1024]{2,1,0:T(8,128)(2,1)S(1)}, u32[]{:S(2)}, u32[]{:S(2)}) async-start(bf16[16,32,1024]{2,1,0:T(8,128)(2,1)} %bitcast.2), calls=%async_computation.2 | async-start | bytes 2097152 | tf_op jit(solution)/shard_map/all_to_all | solution.py:32
  75.9 13.2 %all-to-all-start.3 = ((f32[16,32,1]{1,2,0:T(1,128)}), f32[16,32,1]{1,2,0:T(1,128)S(1)}, u32[]{:S(2)}, u32[]{:S(2)}) async-start(f32[16,32,1]{1,2,0:T(1,128)} %bitcast.4), calls=%async_computation.3 | async-start | bytes 16384 | tf_op jit(solution)/shard_map/all_to_all | solution.py:48
Sparse Core Ops, SparseCore 0:
  13.6 75.8 reduce-scatter.1
where the time goes:
time: 103 us; the launch traced here: 102 us
  waiting for transfers between devices  43.5 us (42%)
  starting transfers between devices  21.4 us (21%)
  between operations  14.1 us (14%)
  other arithmetic  9.53 us (9%)
  local copies, waits for them, and re-layouts  8.9 us (9%)
  matrix products  4.97 us (5%)
    all_to_all x1, waiting for transfers between devices, per_device(): lax.all_to_all(send_rows, 'shard', split_axis=0, concat_axis=0, tiled=True)  29.4 us
    all_to_all x1, starting transfers between devices, per_device(): lax.all_to_all(send_order, 'shard', split_axis=0, concat_axis=0, tiled=True)  7.39 us
    all_to_all x1, starting transfers between devices, per_device(): lax.all_to_all(maxima, 'shard', split_axis=0, concat_axis=0, tiled=True)  6.91 us
    all_to_all x1, waiting for transfers between devices, per_device(): lax.all_to_all(maxima, 'shard', split_axis=0, concat_axis=0, tiled=True)  6.32 us
    all_to_all x1, waiting for transfers between devices, per_device(): lax.all_to_all(send_order, 'shard', split_axis=0, concat_axis=0, tiled=True)  4.1 us
    all_to_all x1, starting transfers between devices, per_device(): lax.all_to_all(send_rows, 'shard', split_axis=0, concat_axis=0, tiled=True)  3.65 us
    all_to_all x1, waiting for transfers between devices, per_device(): lax.all_to_all(send_cluster, 'shard', split_axis=0, concat_axis=0, tiled=...  3.62 us
    all_to_all x1, starting transfers between devices, per_device(): lax.all_to_all(send_cluster, 'shard', split_axis=0, concat_axis=0, tiled=...  3.42 us
  transfers between devices with their start and end apart: 5, of which 4 were waited for; matrix products, arithmetic and copies ran while one was open for 12% of the time, Pallas kernels for 0%

commit v1 on v0

v1 whole, which is shorter than its diff:
```python
import functools

import jax
import jax.numpy as jnp
from jax import lax
from jax.experimental import pallas as pl
from jax.experimental.pallas import tpu as pltpu
from jax.sharding import PartitionSpec as P

CL_DEV = 32
EPSILON = 1e-06
ORDER_SPAN = 32768
MESH = pl.DeviceIdType.MESH
F32 = jnp.float32
BF16 = jnp.bfloat16


def flipped(me, k):
    peer = me
    bit = 1
    while bit <= k:
        if k & bit:
            peer = peer + bit * (1 - 2 * ((me // bit) % 2))
        bit *= 2
    return peer


def exchange_kernel(
    n, cap,
    emb_ref, dest_ref, member_ref, order_ref,
    best_ref, cent_ref,
    unit, pack, send, recv, keys_out, keys_in, best_out, best_in,
    row_send, row_recv, key_send, key_recv, best_send, best_recv,
):
    me = lax.axis_index("shard")
    rows = emb_ref.shape[0]
    features = emb_ref.shape[1]
    slots = n * cap
    per_tile = 128 // cap
    tiles = slots // 128

    barrier = pltpu.get_barrier_semaphore()
    for k in range(1, n):
        pl.semaphore_signal(
            barrier, inc=1, device_id={"shard": flipped(me, k)}, device_id_type=MESH
        )

    dest = dest_ref[...]
    owner_table = (lax.broadcasted_iota(jnp.int32, (n, rows), 0) == dest).astype(F32)
    before = (
        lax.broadcasted_iota(jnp.int32, (rows, rows), 0)
        < lax.broadcasted_iota(jnp.int32, (rows, rows), 1)
    ).astype(F32).astype(BF16)
    earlier = jnp.dot(owner_table.astype(BF16), before, preferred_element_type=F32)
    rank = jnp.sum(earlier * owner_table, axis=0, keepdims=True).astype(jnp.int32)
    slot = jnp.bitwise_xor(dest, me) * cap + rank
    pack[...] = (
        lax.broadcasted_iota(jnp.int32, (slots, rows), 0) == slot
    ).astype(F32).astype(BF16)

    part = lax.broadcasted_iota(jnp.int32, (8, rows), 0)
    order = order_ref[...]
    fields = jnp.where(
        part == 0,
        member_ref[...] + 1,
        jnp.where(part == 1, order // 128, jnp.where(part == 2, order % 128, 0)),
    ).astype(F32).astype(BF16)
    packed = lax.dot_general(
        fields, pack[...], (((1,), (1,)), ((), ())), preferred_element_type=F32
    )
    key_row = packed[0:1] * float(ORDER_SPAN) + packed[1:2] * 128.0 + packed[2:3]
    for t in range(tiles):
        keys_out[t] = jnp.broadcast_to(key_row[:, t * 128:(t + 1) * 128], (8, 128))

    x = emb_ref[...]
    squares = jnp.sum(x * x, axis=1, keepdims=True)
    unit[...] = (x * lax.rsqrt(squares + EPSILON)).astype(BF16)

    pl.semaphore_wait(barrier, n - 1)

    def copy(src, dst, sems, k):
        return pltpu.make_async_remote_copy(
            src_ref=src, dst_ref=dst, send_sem=sems[0].at[k], recv_sem=sems[1].at[k],
            device_id={"shard": flipped(me, k)}, device_id_type=MESH,
        )

    row_copies, key_copies, best_copies = {}, {}, {}
    for t in reversed(range(tiles)):
        block = jnp.dot(
            pack[t * 128:(t + 1) * 128, :], unit[...], preferred_element_type=F32
        ).astype(BF16)
        send[t * 128:(t + 1) * 128, :] = block
        for k in reversed(range(t * per_tile, (t + 1) * per_tile)):
            if k == 0:
                recv[0:cap, :] = block[0:cap, :]
                continue
            key_copies[k] = copy(keys_out.at[t], keys_in.at[k], (key_send, key_recv), k)
            row_copies[k] = copy(
                send.at[pl.ds(k * cap, cap)], recv.at[pl.ds(k * cap, cap)],
                (row_send, row_recv), k,
            )
            key_copies[k].start()
            row_copies[k].start()

    lane = lax.broadcasted_iota(jnp.int32, (8, 128), 1) // cap

    def gathered(own, arrived):
        result = []
        for t in range(tiles):
            tile = own[t] if t == 0 else arrived[t * per_tile]
            for j in range(1, per_tile):
                tile = jnp.where(lane == j, arrived[t * per_tile + j], tile)
            result.append(tile)
        return result

    for k in range(1, n):
        key_copies[k].wait_recv()
    key_tiles = gathered(keys_out, keys_in)
    key_lanes = jnp.concatenate([tile[0:1] for tile in key_tiles], axis=1)
    cluster_lanes = jnp.floor(key_lanes * (1.0 / ORDER_SPAN))
    base_lanes = cluster_lanes * float(ORDER_SPAN)
    key_cols = [
        jnp.transpose(jnp.broadcast_to(tile[0:1], (128, 128)))[:, 0:1] for tile in key_tiles
    ]

    for k in range(1, n):
        row_copies[k].wait_recv()

    best = jnp.full((1, slots), -1.0, F32)
    for t in range(tiles):
        scores = lax.dot_general(
            recv[t * 128:(t + 1) * 128, :], recv[...], (((1,), (1,)), ((), ())),
            preferred_element_type=F32,
        )
        column = jnp.broadcast_to(key_cols[t], (128, slots))
        allowed = (column < key_lanes) & (column >= base_lanes)
        best = jnp.maximum(
            best, jnp.max(jnp.where(allowed, scores, -1.0), axis=0, keepdims=True)
        )
    for t in range(tiles):
        best_out[t] = jnp.broadcast_to(best[:, t * 128:(t + 1) * 128], (8, 128))
    for k in range(1, n):
        best_copies[k] = copy(
            best_out.at[k // per_tile], best_in.at[k], (best_send, best_recv), k
        )
        best_copies[k].start()

    clusters = cent_ref.shape[0]
    wanted = lax.broadcasted_iota(jnp.int32, (clusters, slots), 0).astype(F32) + 1.0
    member_table = (wanted == cluster_lanes).astype(F32).astype(BF16)
    sums = jnp.dot(member_table, recv[...], preferred_element_type=F32)
    cent_ref[...] = sums * lax.rsqrt(
        jnp.sum(sums * sums, axis=1, keepdims=True) * (1.0 / features) + EPSILON
    )

    for k in range(1, n):
        best_copies[k].wait_recv()
    returned = jnp.concatenate(gathered(best_out, best_in), axis=1)
    result = jnp.zeros((8, rows), F32)
    pieces = []
    for _ in range(3):
        piece = returned.astype(BF16)
        pieces.append(piece)
        returned = returned - piece.astype(F32)
    for piece in pieces:
        result = result + jnp.dot(piece, pack[...], preferred_element_type=F32)
    best_ref[...] = result[0:1]

    for k in range(1, n):
        key_copies[k].wait_send()
        row_copies[k].wait_send()
        best_copies[k].wait_send()


def fused(embeddings, dest_owner, member_cluster, order, n, cap):
    rows, features = embeddings.shape
    slots = n * cap
    vmem = pl.BlockSpec(memory_space=pltpu.VMEM)
    best, centroids = pl.pallas_call(
        functools.partial(exchange_kernel, n, cap),
        out_shape=(
            jax.ShapeDtypeStruct((1, rows), F32),
            jax.ShapeDtypeStruct((CL_DEV, features), F32),
        ),
        in_specs=[vmem] * 4,
        out_specs=(vmem, vmem),
        scratch_shapes=[
            pltpu.VMEM((rows, features), BF16),
            pltpu.VMEM((slots, rows), BF16),
            pltpu.VMEM((slots, features), BF16),
            pltpu.VMEM((slots, features), BF16),
            pltpu.VMEM((slots // 128, 8, 128), F32),
            pltpu.VMEM((n, 8, 128), F32),
            pltpu.VMEM((slots // 128, 8, 128), F32),
            pltpu.VMEM((n, 8, 128), F32),
        ] + [pltpu.SemaphoreType.DMA((n,))] * 6,
        compiler_params=pltpu.CompilerParams(
            collective_id=0, has_side_effects=True, vmem_limit_bytes=32 * 1024 * 1024
        ),
        cost_estimate=pl.CostEstimate(
            flops=2 * slots * features * (rows + slots + CL_DEV),
            bytes_accessed=4 * rows * features,
            transcendentals=rows,
        ),
    )(
        embeddings,
        dest_owner.reshape(1, rows),
        member_cluster.reshape(1, rows),
        order.reshape(1, rows),
    )
    return best.reshape(rows), centroids


def plain(embeddings, dest_owner, member_cluster, order, owners, capacity):
    rows_here, features = embeddings.shape
    slots = owners * capacity
    squares = jnp.sum(embeddings * embeddings, axis=1, keepdims=True)
    unit_rows = (embeddings * lax.rsqrt(squares + EPSILON)).astype(BF16)
    owner_table = (dest_owner[:, None] == jnp.arange(owners, dtype=jnp.int32)[None, :]).astype(F32)
    positions = jnp.arange(rows_here, dtype=jnp.int32)
    before = (positions[:, None] > positions[None, :]).astype(F32)
    earlier = jnp.dot(before, owner_table, precision=lax.Precision.HIGHEST)
    rank = jnp.sum(earlier * owner_table, axis=1).astype(jnp.int32)
    slot_index = dest_owner * capacity + rank
    send_rows = jnp.zeros((slots, features), BF16).at[slot_index].set(unit_rows)
    code = (member_cluster + 1) * ORDER_SPAN + order
    send_code = jnp.zeros((slots,), jnp.int32).at[slot_index].set(code)
    recv_rows = lax.all_to_all(send_rows, "shard", split_axis=0, concat_axis=0, tiled=True)
    recv_code = lax.all_to_all(send_code, "shard", split_axis=0, concat_axis=0, tiled=True)
    recv_cluster = recv_code // ORDER_SPAN
    scores = lax.dot_general(
        recv_rows, recv_rows, (((1,), (1,)), ((), ())), preferred_element_type=F32
    )
    allowed = (recv_cluster[:, None] == recv_cluster[None, :]) & (
        recv_code[None, :] < recv_code[:, None]
    )
    maxima = jnp.max(jnp.where(allowed, scores, F32(-1.0)), axis=1)
    returned = lax.all_to_all(maxima, "shard", split_axis=0, concat_axis=0, tiled=True)
    max_similarity = returned[slot_index]
    wanted = jnp.arange(CL_DEV, dtype=jnp.int32) + 1
    member_table = (wanted[:, None] == recv_cluster[None, :]).astype(BF16)
    sums = jnp.dot(member_table, recv_rows, preferred_element_type=F32)
    centroids = sums * lax.rsqrt(jnp.mean(sums * sums, axis=1, keepdims=True) + EPSILON)
    return (max_similarity, centroids)


def per_device(embeddings, dest_owner, member_cluster, order):
    owners = lax.axis_size("shard")
    capacity = 2 * embeddings.shape[0] // owners
    blocks_tile = capacity % 16 == 0 and 128 % capacity == 0 and owners & (owners - 1) == 0
    body = fused if blocks_tile else plain
    return body(embeddings, dest_owner, member_cluster, order, owners, capacity)


def solution(mesh):
    in_specs = (
        P(("groups", "shard"), None),
        P(("groups", "shard")),
        P(("groups", "shard")),
        P(("groups", "shard")),
    )
    out_specs = (P(("groups", "shard")), P(("groups", "shard"), None))
    return jax.shard_map(
        per_device, mesh=mesh, in_specs=in_specs, out_specs=out_specs, check_vma=False
    )
```

time: 103 us -> 43.7 us (0.42)
  waiting for transfers between devices: 43.5 us -> 0 us
  Pallas kernels: 0 us -> 39.8 us
  starting transfers between devices: 21.4 us -> 0 us
  between operations: 14.1 us -> 0.67 us
  other arithmetic: 9.53 us -> 0 us
  local copies, waits for them, and re-layouts: 8.9 us -> 3.13 us
  matrix products: 4.97 us -> 0 us
    all_to_all x4 -> x0, waiting for transfers between devices: 43.5 us -> none  [the longest x1 29.4 us: per_device(): lax.all_to_all(send_rows, 'shard', split_axis=0, concat_axis=0, tiled=True)]
    pallas_call x0 -> x1, Pallas kernels: none -> 39.8 us  [fused(): pl.pallas_call(functools.partial(exchange_kernel, n, cap), out_shape=(jax...]
    all_to_all x4 -> x0, starting transfers between devices: 21.4 us -> none  [the longest x1 7.39 us: per_device(): lax.all_to_all(send_order, 'shard', split_axis=0, concat_axis=0, tiled=True)]
    dot_general x3 -> x0, matrix products: 4.97 us -> none  [the longest x1 3.19 us: per_device(): jnp.dot(member_table, unit_rows, preferred_element_type=jnp.float32)]
    all_to_all x6 -> x0, local copies, waits for them, and re-layouts: 3.13 us -> none  [the longest x3 1.27 us: per_device(): lax.all_to_all(maxima, 'shard', split_axis=0, concat_axis=0, tiled=True)]
    unnamed x2 -> x10, local copies, waits for them, and re-layouts: 0.01 us -> 3.13 us
    scatter x2 -> x0, local copies, waits for them, and re-layouts: 3.1 us -> none  [the longest x1 1.55 us: per_device(): send_order = jnp.zeros((slots,), jnp.int32).at[slot_index].set(order)]
    scatter x1 -> x0, other arithmetic: 2.72 us -> none  [per_device(): jnp.zeros((slots, features), jnp.bfloat16).at[slot_index].set(unit_rows)]
  transfers between devices with their start and end apart: 5 -> 0, of which waited for: 4 -> 0; matrix products, arithmetic and copies ran while one was open for 12% -> 0% of each run, Pallas kernels for 0% -> 0%
where the time goes in v1:
time: 43.7 us; the launch traced here: 43.6 us
  Pallas kernels  39.8 us (91%)
  local copies, waits for them, and re-layouts  3.13 us (7%)
  between operations  0.67 us (2%)
    pallas_call x1, Pallas kernels, fused(): pl.pallas_call(functools.partial(exchange_kernel, n, cap), out_shape=(jax...  39.8 us
    unnamed x10, local copies, waits for them, and re-layouts  3.13 us

profile of v1, /device:TPU:0, one launch (start us, length us, event | category | flops | bytes accessed | tf_op | source)
XLA Modules:
  0.0 43.6 jit_solution(13233677693227669940)
XLA Ops:
  0.6 0.0 copy-start.2
  0.6 0.0 copy-start.3
  0.7 0.0 copy-start.1
  0.7 0.7 %copy-done.2 = s32[256]{0:T(256)S(1)} copy-done((s32[256]{0:T(256)S(1)}, s32[256]{0:T(256)}, u32[]{:S(2)}) %copy-start.2) | copy-done | bytes 1048
  1.3 0.0 copy-done.3
  1.3 0.0 copy-done.1
  1.3 0.0 copy-start
  1.3 1.2 %copy-done = f32[256,1024]{1,0:T(8,128)S(1)} copy-done((f32[256,1024]{1,0:T(8,128)S(1)}, f32[256,1024]{1,0:T(8,128)}, u32[]{:S(2)}) %copy-start) | copy-done | bytes 1048600
  2.6 39.8 %shard_map.59 = (f32[1,256]{1,0:T(1,128)S(1)}, f32[32,1024]{1,0:T(8,128)S(1)}) custom-call(f32[256,1024]{1,0:T(8,128)S(1)} %copy-done, s32[1,256]{1,0:T(1,128)S(1)} %bitcast.5, s32[1,256]{1,0:T(1,128)S(1)} %bitcast.6, s32[1,256]{1,0:T(1,128)S(1)} %bitcast.7), custom_call_target="tpu_custom_call" | custom-call | flops 838860800 | bytes 1048576 | tf_op jit(solution)/shard_map/pallas_call | solution.py:179
  42.3 0.6 %copy.8 = f32[256]{0:T(256)} copy(f32[256]{0:T(256)S(1)} %bitcast.4) | data formatting | bytes 2048
  42.9 0.7 %copy.9 = f32[32,1024]{1,0:T(8,128)} copy(f32[32,1024]{1,0:T(8,128)S(1)} %get-tuple-element.9) | data formatting | bytes 262144
Async XLA Ops:
  0.6 0.7 %copy-start.2 = (s32[256]{0:T(256)S(1)}, s32[256]{0:T(256)}, u32[]{:S(2)}) copy-start(s32[256]{0:T(256)} %param.6) | copy-start | bytes 3076
  0.6 0.7 %copy-start.3 = (s32[256]{0:T(256)S(1)}, s32[256]{0:T(256)}, u32[]{:S(2)}) copy-start(s32[256]{0:T(256)} %param.7) | copy-start | bytes 3076
  0.7 0.7 %copy-start.1 = (s32[256]{0:T(256)S(1)}, s32[256]{0:T(256)}, u32[]{:S(2)}) copy-start(s32[256]{0:T(256)} %param.5) | copy-start | bytes 3076
  1.3 1.2 %copy-start = (f32[256,1024]{1,0:T(8,128)S(1)}, f32[256,1024]{1,0:T(8,128)}, u32[]{:S(2)}) copy-start(f32[256,1024]{1,0:T(8,128)} %emb_ref.1) | copy-start | bytes 3145732

commit v2 on v1

--- a/solution.py
+++ b/solution.py
@@ -15,24 +15,39 @@
 BF16 = jnp.bfloat16
 
 
-def flipped(me, k):
-    peer = me
+def flipped(me, n):
+    steps = []
     bit = 1
-    while bit <= k:
-        if k & bit:
-            peer = peer + bit * (1 - 2 * ((me // bit) % 2))
+    while bit < n:
+        steps.append(bit * (1 - 2 * lax.rem(lax.div(me, bit), 2)))
         bit *= 2
-    return peer
+    peers = [me]
+    for step in steps:
+        peers = peers + [peer + step for peer in peers]
+    return peers
 
 
 def exchange_kernel(
     n, cap,
-    emb_ref, dest_ref, member_ref, order_ref,
+    emb_hbm, dest_hbm, member_hbm, order_hbm,
     best_ref, cent_ref,
     unit, pack, send, recv, keys_out, keys_in, best_out, best_in,
     row_send, row_recv, key_send, key_recv, best_send, best_recv,
+    emb_ref, dest_ref, member_ref, order_ref, load_sem,
 ):
     me = lax.axis_index("shard")
+    peers = flipped(me, n)
+    loads = [
+        pltpu.make_async_copy(src, dst, load_sem.at[i])
+        for i, (src, dst) in enumerate(
+            [
+                (dest_hbm, dest_ref), (member_hbm, member_ref), (order_hbm, order_ref),
+                (emb_hbm, emb_ref),
+            ]
+        )
+    ]
+    for load in loads:
+        load.start()
     rows = emb_ref.shape[0]
     features = emb_ref.shape[1]
     slots = n * cap
@@ -42,9 +57,11 @@
     barrier = pltpu.get_barrier_semaphore()
     for k in range(1, n):
         pl.semaphore_signal(
-            barrier, inc=1, device_id={"shard": flipped(me, k)}, device_id_type=MESH
-        )
-
+            barrier, inc=1, device_id={"shard": peers[k]}, device_id_type=MESH
+        )
+
+    for load in loads[:3]:
+        load.wait()
     dest = dest_ref[...]
     owner_table = (lax.broadcasted_iota(jnp.int32, (n, rows), 0) == dest).astype(F32)
     before = (
@@ -72,6 +89,7 @@
     for t in range(tiles):
         keys_out[t] = jnp.broadcast_to(key_row[:, t * 128:(t + 1) * 128], (8, 128))
 
+    loads[3].wait()
     x = emb_ref[...]
     squares = jnp.sum(x * x, axis=1, keepdims=True)
     unit[...] = (x * lax.rsqrt(squares + EPSILON)).astype(BF16)
@@ -81,26 +99,30 @@
     def copy(src, dst, sems, k):
         return pltpu.make_async_remote_copy(
             src_ref=src, dst_ref=dst, send_sem=sems[0].at[k], recv_sem=sems[1].at[k],
-            device_id={"shard": flipped(me, k)}, device_id_type=MESH,
+            device_id={"shard": peers[k]}, device_id_type=MESH,
         )
 
     row_copies, key_copies, best_copies = {}, {}, {}
-    for t in reversed(range(tiles)):
+    for step, t in enumerate(range(tiles)):
         block = jnp.dot(
             pack[t * 128:(t + 1) * 128, :], unit[...], preferred_element_type=F32
         ).astype(BF16)
         send[t * 128:(t + 1) * 128, :] = block
-        for k in reversed(range(t * per_tile, (t + 1) * per_tile)):
+        for k in range(t * per_tile, (t + 1) * per_tile):
             if k == 0:
                 recv[0:cap, :] = block[0:cap, :]
                 continue
-            key_copies[k] = copy(keys_out.at[t], keys_in.at[k], (key_send, key_recv), k)
             row_copies[k] = copy(
                 send.at[pl.ds(k * cap, cap)], recv.at[pl.ds(k * cap, cap)],
                 (row_send, row_recv), k,
             )
-            key_copies[k].start()
             row_copies[k].start()
+        if step == 0:
+            for k in range(1, n):
+                key_copies[k] = copy(
+                    keys_out.at[k // per_tile], keys_in.at[k], (key_send, key_recv), k
+                )
+                key_copies[k].start()
 
     lane = lax.broadcasted_iota(jnp.int32, (8, 128), 1) // cap
 
@@ -123,20 +145,33 @@
         jnp.transpose(jnp.broadcast_to(tile[0:1], (128, 128)))[:, 0:1] for tile in key_tiles
     ]
 
-    for k in range(1, n):
-        row_copies[k].wait_recv()
-
-    best = jnp.full((1, slots), -1.0, F32)
+    def tile_max(scores, column, lanes):
+        keys, bases = key_lanes[:, lanes], base_lanes[:, lanes]
+        column = jnp.broadcast_to(column, scores.shape)
+        allowed = (column < keys) & (column >= bases)
+        return jnp.max(jnp.where(allowed, scores, -1.0), axis=0, keepdims=True)
+
+    def inner(a, b):
+        return lax.dot_general(
+            a, b, (((1,), (1,)), ((), ())), preferred_element_type=F32
+        )
+
+    best = None
     for t in range(tiles):
-        scores = lax.dot_general(
-            recv[t * 128:(t + 1) * 128, :], recv[...], (((1,), (1,)), ((), ())),
-            preferred_element_type=F32,
-        )
-        column = jnp.broadcast_to(key_cols[t], (128, slots))
-        allowed = (column < key_lanes) & (column >= base_lanes)
-        best = jnp.maximum(
-            best, jnp.max(jnp.where(allowed, scores, -1.0), axis=0, keepdims=True)
-        )
+        for k in range(max(1, t * per_tile), (t + 1) * per_tile):
+            row_copies[k].wait_recv()
+        head, here = t * 128, slice(t * 128, (t + 1) * 128)
+        ours = tile_max(
+            inner(recv[0:head + 128, :], recv[here, :]),
+            jnp.concatenate(key_cols[:t + 1], axis=0), here,
+        )
+        if t == 0:
+            best = ours
+        else:
+            theirs = tile_max(
+                inner(recv[here, :], recv[0:head, :]), key_cols[t], slice(0, head)
+            )
+            best = jnp.concatenate([jnp.maximum(best, theirs), ours], axis=1)
     for t in range(tiles):
         best_out[t] = jnp.broadcast_to(best[:, t * 128:(t + 1) * 128], (8, 128))
     for k in range(1, n):
@@ -182,7 +217,7 @@
             jax.ShapeDtypeStruct((1, rows), F32),
             jax.ShapeDtypeStruct((CL_DEV, features), F32),
         ),
-        in_specs=[vmem] * 4,
+        in_specs=[pl.BlockSpec(memory_space=pltpu.HBM)] * 4,
         out_specs=(vmem, vmem),
         scratch_shapes=[
             pltpu.VMEM((rows, features), BF16),
@@ -193,7 +228,13 @@
             pltpu.VMEM((n, 8, 128), F32),
             pltpu.VMEM((slots // 128, 8, 128), F32),
             pltpu.VMEM((n, 8, 128), F32),
-        ] + [pltpu.SemaphoreType.DMA((n,))] * 6,
+        ] + [pltpu.SemaphoreType.DMA((n,))] * 6 + [
+            pltpu.VMEM((rows, features), F32),
+            pltpu.VMEM((1, rows), jnp.int32),
+            pltpu.VMEM((1, rows), jnp.int32),
+            pltpu.VMEM((1, rows), jnp.int32),
+            pltpu.SemaphoreType.DMA((4,)),
+        ],
         compiler_params=pltpu.CompilerParams(
             collective_id=0, has_side_effects=True, vmem_limit_bytes=32 * 1024 * 1024
         ),

time: 43.7 us -> 42.2 us (0.966)
  Pallas kernels: 39.8 us -> 38.2 us
    pallas_call x1, Pallas kernels: 39.8 us -> 38.2 us  [fused(): pl.pallas_call(functools.partial(exchange_kernel, n, cap), out_shape=(jax...]
where the time goes in v2:
time: 42.2 us; the launch traced here: 42 us
  Pallas kernels  38.2 us (91%)
  local copies, waits for them, and re-layouts  3.13 us (7%)
  between operations  0.67 us (2%)
    pallas_call x1, Pallas kernels, fused(): pl.pallas_call(functools.partial(exchange_kernel, n, cap), out_shape=(jax...  38.2 us
    unnamed x10, local copies, waits for them, and re-layouts  3.13 us

profile of v2, /device:TPU:0, one launch (start us, length us, event | category | flops | bytes accessed | tf_op | source)
XLA Modules:
  0.0 42.0 jit_solution(16020319920618965293)
XLA Ops:
  0.6 0.0 copy-start.2
  0.6 0.0 copy-start.3
  0.7 0.0 copy-start.1
  0.7 0.7 %copy-done.2 = s32[256]{0:T(256)S(1)} copy-done((s32[256]{0:T(256)S(1)}, s32[256]{0:T(256)}, u32[]{:S(2)}) %copy-start.2) | copy-done | bytes 1048
  1.3 0.0 copy-done.3
  1.3 0.0 copy-done.1
  1.3 0.0 copy-start
  1.3 1.2 %copy-done = f32[256,1024]{1,0:T(8,128)S(1)} copy-done((f32[256,1024]{1,0:T(8,128)S(1)}, f32[256,1024]{1,0:T(8,128)}, u32[]{:S(2)}) %copy-start) | copy-done | bytes 1048600
  2.6 38.2 %shard_map.59 = (f32[1,256]{1,0:T(1,128)S(1)}, f32[32,1024]{1,0:T(8,128)S(1)}) custom-call(f32[256,1024]{1,0:T(8,128)S(1)} %copy-done, s32[1,256]{1,0:T(1,128)S(1)} %bitcast.5, s32[1,256]{1,0:T(1,128)S(1)} %bitcast.6, s32[1,256]{1,0:T(1,128)S(1)} %bitcast.7), custom_call_target="tpu_custom_call" | custom-call | flops 838860800 | bytes 1048576 | tf_op jit(solution)/shard_map/pallas_call | solution.py:214
  40.8 0.6 %copy.8 = f32[256]{0:T(256)} copy(f32[256]{0:T(256)S(1)} %bitcast.4) | data formatting | bytes 2048
  41.3 0.7 %copy.9 = f32[32,1024]{1,0:T(8,128)} copy(f32[32,1024]{1,0:T(8,128)S(1)} %get-tuple-element.9) | data formatting | bytes 262144
Async XLA Ops:
  0.6 0.7 %copy-start.2 = (s32[256]{0:T(256)S(1)}, s32[256]{0:T(256)}, u32[]{:S(2)}) copy-start(s32[256]{0:T(256)} %param.6) | copy-start | bytes 3076
  0.6 0.7 %copy-start.3 = (s32[256]{0:T(256)S(1)}, s32[256]{0:T(256)}, u32[]{:S(2)}) copy-start(s32[256]{0:T(256)} %param.7) | copy-start | bytes 3076
  0.7 0.7 %copy-start.1 = (s32[256]{0:T(256)S(1)}, s32[256]{0:T(256)}, u32[]{:S(2)}) copy-start(s32[256]{0:T(256)} %param.5) | copy-start | bytes 3076
  1.3 1.2 %copy-start = (f32[256,1024]{1,0:T(8,128)S(1)}, f32[256,1024]{1,0:T(8,128)}, u32[]{:S(2)}) copy-start(f32[256,1024]{1,0:T(8,128)} %emb_hbm.1) | copy-start | bytes 3145732

commit v3 on v2

--- a/solution.py
+++ b/solution.py
@@ -10,6 +10,7 @@
 CL_DEV = 32
 EPSILON = 1e-06
 ORDER_SPAN = 32768
+OVER = 48
 MESH = pl.DeviceIdType.MESH
 F32 = jnp.float32
 BF16 = jnp.bfloat16
@@ -25,6 +26,282 @@
     for step in steps:
         peers = peers + [peer + step for peer in peers]
     return peers
+
+
+def relay_kernel(
+    n, cap,
+    emb_hbm, dest_hbm, member_hbm, order_hbm,
+    best_ref, cent_ref, flag_ref,
+    unit, pack, send, recv, keys_out, keys_in, best_out, best_in,
+    row_send, row_recv, key_send, key_recv, best_send, best_recv,
+    emb_ref, dest_ref, member_ref, order_ref, load_sem,
+    over_out, over_in, place_out, place_in, relay, flag_out, flag_in,
+    over_sem, place_sem, relay_send, relay_recv, flag_sem,
+):
+    me = lax.axis_index("shard")
+    peers = flipped(me, n)
+    loads = [
+        pltpu.make_async_copy(src, dst, load_sem.at[i])
+        for i, (src, dst) in enumerate(
+            [
+                (dest_hbm, dest_ref), (member_hbm, member_ref), (order_hbm, order_ref),
+                (emb_hbm, emb_ref),
+            ]
+        )
+    ]
+    for load in loads:
+        load.start()
+    rows = emb_ref.shape[0]
+    features = emb_ref.shape[1]
+    slots = n * cap
+    per_tile = 128 // cap
+    half, part_cap = n // 2, cap // 2
+    tiles = slots // 128
+
+    barrier = pltpu.get_barrier_semaphore()
+    for k in range(1, n):
+        pl.semaphore_signal(
+            barrier, inc=1, device_id={"shard": peers[k]}, device_id_type=MESH
+        )
+
+    across = {"groups": 1 - lax.axis_index("groups")}
+    pl.semaphore_signal(barrier, inc=1, device_id=across, device_id_type=MESH)
+
+    for load in loads[:3]:
+        load.wait()
+    dest = dest_ref[...]
+    owner_table = (lax.broadcasted_iota(jnp.int32, (n, rows), 0) == dest).astype(F32)
+    before = (
+        lax.broadcasted_iota(jnp.int32, (rows, rows), 0)
+        < lax.broadcasted_iota(jnp.int32, (rows, rows), 1)
+    ).astype(F32).astype(BF16)
+    earlier = jnp.dot(owner_table.astype(BF16), before, preferred_element_type=F32)
+    rank = jnp.sum(earlier * owner_table, axis=0, keepdims=True).astype(jnp.int32)
+    hop = jnp.bitwise_xor(dest, me)
+    over = (hop >= half) & (rank >= part_cap)
+    slot = jnp.where(
+        hop < half,
+        hop * cap + rank,
+        half * cap + (hop - half) * part_cap + rank
+        + jnp.where(over, half * part_cap - part_cap, 0),
+    )
+    over_row = over.astype(F32)
+    over_rank = jnp.dot(
+        jnp.broadcast_to(over_row, (8, rows)).astype(BF16), before,
+        preferred_element_type=F32,
+    )[0:1]
+    over_count = jnp.sum(over_row, axis=1, keepdims=True)
+    flag = (over_count > float(OVER)).astype(F32)
+    pick = (
+        (lax.broadcasted_iota(jnp.int32, (128, rows), 0).astype(F32) == over_rank)
+        & (over_row > 0.5)
+    ).astype(F32).astype(BF16)
+    place = (hop - half) * part_cap + rank - part_cap + 1
+    place = lax.dot_general(
+        jnp.broadcast_to(place, (8, rows)).astype(F32).astype(BF16), pick,
+        (((1,), (1,)), ((), ())), preferred_element_type=F32,
+    )
+    place_out[...] = place - 1.0
+    pack[...] = (
+        lax.broadcasted_iota(jnp.int32, (slots, rows), 0) == slot
+    ).astype(F32).astype(BF16)
+
+    part = lax.broadcasted_iota(jnp.int32, (8, rows), 0)
+    order = order_ref[...]
+    fields = jnp.where(
+        part == 0,
+        member_ref[...] + 1,
+        jnp.where(part == 1, order // 128, jnp.where(part == 2, order % 128, 0)),
+    ).astype(F32).astype(BF16)
+    packed = lax.dot_general(
+        fields, pack[...], (((1,), (1,)), ((), ())), preferred_element_type=F32
+    )
+    key_row = packed[0:1] * float(ORDER_SPAN) + packed[1:2] * 128.0 + packed[2:3]
+    for t in range(tiles):
+        keys_out[t] = jnp.where(
+            lax.broadcasted_iota(jnp.int32, (8, 128), 0) == 0,
+            jnp.broadcast_to(key_row[:, t * 128:(t + 1) * 128], (8, 128)),
+            jnp.broadcast_to(flag, (8, 128)),
+        )
+
+    loads[3].wait()
+    x = emb_ref[...]
+    squares = jnp.sum(x * x, axis=1, keepdims=True)
+    unit[...] = (x * lax.rsqrt(squares + EPSILON)).astype(BF16)
+
+    pl.semaphore_wait(barrier, n)
+
+    def copy(src, dst, sends, recvs, k):
+        return pltpu.make_async_remote_copy(
+            src_ref=src, dst_ref=dst, send_sem=sends, recv_sem=recvs,
+            device_id={"shard": peers[k]}, device_id_type=MESH,
+        )
+
+    def tiles_of(k):
+        return (k // per_tile, 1) if k < half else (2, 2)
+
+    def rows_of(k):
+        if k < half:
+            return pl.ds(k * cap, cap)
+        return pl.ds(half * cap + (k - half) * part_cap, part_cap)
+
+    over_out[...] = jnp.dot(
+        pick[0:OVER, :], unit[...], preferred_element_type=F32
+    ).astype(BF16)
+    over_copy = copy(over_out, over_in, over_sem.at[0], over_sem.at[1], half)
+    place_copy = copy(place_out, place_in, place_sem.at[0], place_sem.at[1], half)
+    place_copy.start()
+    over_copy.start()
+    row_copies, key_copies, best_copies, relays = {}, {}, {}, {}
+    for step, t in enumerate((2, 0, 1)):
+        block = jnp.dot(
+            pack[t * 128:(t + 1) * 128, :], unit[...], preferred_element_type=F32
+        ).astype(BF16)
+        send[t * 128:(t + 1) * 128, :] = block
+        if t == 0:
+            recv[0:cap, :] = block[0:cap, :]
+        for k in range(1, n):
+            if tiles_of(k)[0] != t:
+                continue
+            row_copies[k] = copy(
+                send.at[rows_of(k)], recv.at[rows_of(k)],
+                row_send.at[k], row_recv.at[k], k,
+            )
+            row_copies[k].start()
+        if step == 0:
+            for k in range(1, n):
+                first, count = tiles_of(k)
+                key_copies[k] = copy(
+                    keys_out.at[pl.ds(first, count)], keys_in.at[k, pl.ds(0, count)],
+                    key_send.at[k], key_recv.at[k], k,
+                )
+                key_copies[k].start()
+
+    place_copy.wait_recv()
+    over_copy.wait_recv()
+    spread = (
+        lax.broadcasted_iota(jnp.int32, (128, OVER), 0).astype(F32)
+        == place_in[0:1, 0:OVER]
+    ).astype(F32).astype(BF16)
+    block = jnp.dot(spread, over_in[...], preferred_element_type=F32).astype(BF16)
+    relay[...] = block
+    extra = 3 * 128
+    recv[extra:extra + part_cap, :] = block[0:part_cap, :]
+    for k in range(1, half):
+        relays[k] = copy(
+            relay.at[pl.ds(k * part_cap, part_cap)],
+            recv.at[pl.ds(extra + k * part_cap, part_cap)],
+            relay_send.at[k], relay_recv.at[k], k,
+        )
+        relays[k].start()
+
+    lane = lax.broadcasted_iota(jnp.int32, (8, 128), 1)
+
+    def gathered(own, arrived):
+        result = []
+        for t in range(2):
+            tile = own[t] if t == 0 else arrived[t * per_tile, 0]
+            for j in range(1, per_tile):
+                tile = jnp.where(lane // cap == j, arrived[t * per_tile + j, 0], tile)
+            result.append(tile)
+        for t in range(2):
+            tile = arrived[half, t]
+            for j in range(1, half):
+                tile = jnp.where(lane // part_cap == j, arrived[half + j, t], tile)
+            result.append(tile)
+        return result
+
+    for k in range(1, n):
+        key_copies[k].wait_recv()
+    key_tiles = gathered(keys_out, keys_in)
+    seen = keys_out[0]
+    for k in range(1, n):
+        seen = jnp.maximum(seen, keys_in[k, 0])
+    flag_out[...] = jnp.broadcast_to(seen[1:2], (8, 128))
+    flag_copy = pltpu.make_async_remote_copy(
+        src_ref=flag_out, dst_ref=flag_in, send_sem=flag_sem.at[0],
+        recv_sem=flag_sem.at[1], device_id=across, device_id_type=MESH,
+    )
+    flag_copy.start()
+    key_lanes = jnp.concatenate([tile[0:1] for tile in key_tiles], axis=1)
+    cluster_lanes = jnp.floor(key_lanes * (1.0 / ORDER_SPAN))
+    base_lanes = cluster_lanes * float(ORDER_SPAN)
+    key_cols = [
+        jnp.transpose(jnp.broadcast_to(tile[0:1], (128, 128)))[:, 0:1] for tile in key_tiles
+    ]
+
+    def tile_max(scores, column, lanes):
+        keys, bases = key_lanes[:, lanes], base_lanes[:, lanes]
+        column = jnp.broadcast_to(column, scores.shape)
+        allowed = (column < keys) & (column >= bases)
+        return jnp.max(jnp.where(allowed, scores, -1.0), axis=0, keepdims=True)
+
+    def inner(a, b):
+        return lax.dot_general(
+            a, b, (((1,), (1,)), ((), ())), preferred_element_type=F32
+        )
+
+    best = None
+    for t in range(tiles):
+        if t == 3:
+            for k in range(1, half):
+                relays[k].wait_recv()
+        for k in range(1, n):
+            if tiles_of(k)[0] == t:
+                row_copies[k].wait_recv()
+        head, here = t * 128, slice(t * 128, (t + 1) * 128)
+        ours = tile_max(
+            inner(recv[0:head + 128, :], recv[here, :]),
+            jnp.concatenate(key_cols[:t + 1], axis=0), here,
+        )
+        if t == 0:
+            best = ours
+        else:
+            theirs = tile_max(
+                inner(recv[here, :], recv[0:head, :]), key_cols[t], slice(0, head)
+            )
+            best = jnp.concatenate([jnp.maximum(best, theirs), ours], axis=1)
+    for t in range(tiles):
+        best_out[t] = jnp.broadcast_to(best[:, t * 128:(t + 1) * 128], (8, 128))
+    for k in range(1, n):
+        first, count = tiles_of(k)
+        best_copies[k] = copy(
+            best_out.at[pl.ds(first, count)], best_in.at[k, pl.ds(0, count)],
+            best_send.at[k], best_recv.at[k], k,
+        )
+        best_copies[k].start()
+
+    clusters = cent_ref.shape[0]
+    wanted = lax.broadcasted_iota(jnp.int32, (clusters, slots), 0).astype(F32) + 1.0
+    member_table = (wanted == cluster_lanes).astype(F32).astype(BF16)
+    sums = jnp.dot(member_table, recv[...], preferred_element_type=F32)
+    cent_ref[...] = sums * lax.rsqrt(
+        jnp.sum(sums * sums, axis=1, keepdims=True) * (1.0 / features) + EPSILON
+    )
+
+    for k in range(1, n):
+        best_copies[k].wait_recv()
+    returned = jnp.concatenate(gathered(best_out, best_in), axis=1)
+    result = jnp.zeros((8, rows), F32)
+    pieces = []
+    for _ in range(3):
+        piece = returned.astype(BF16)
+        pieces.append(piece)
+        returned = returned - piece.astype(F32)
+    for piece in pieces:
+        result = result + jnp.dot(piece, pack[...], preferred_element_type=F32)
+    best_ref[...] = result[0:1]
+    flag_copy.wait()
+    flag_ref[...] = jnp.maximum(flag_out[...], flag_in[...])
+    over_copy.wait_send()
+    place_copy.wait_send()
+    for k in range(1, half):
+        relays[k].wait_send()
+
+    for k in range(1, n):
+        key_copies[k].wait_send()
+        row_copies[k].wait_send()
+        best_copies[k].wait_send()
 
 
 def exchange_kernel(
@@ -252,6 +529,68 @@
     return best.reshape(rows), centroids
 
 
+def relayed(embeddings, dest_owner, member_cluster, order, n, cap):
+    rows, features = embeddings.shape
+    slots = n * cap
+    vmem = pl.BlockSpec(memory_space=pltpu.VMEM)
+    best, centroids, flag = pl.pallas_call(
+        functools.partial(relay_kernel, n, cap),
+        out_shape=(
+            jax.ShapeDtypeStruct((1, rows), F32),
+            jax.ShapeDtypeStruct((CL_DEV, features), F32),
+            jax.ShapeDtypeStruct((8, 128), F32),
+        ),
+        in_specs=[pl.BlockSpec(memory_space=pltpu.HBM)] * 4,
+        out_specs=(vmem, vmem, vmem),
+        scratch_shapes=[
+            pltpu.VMEM((rows, features), BF16),
+            pltpu.VMEM((slots, rows), BF16),
+            pltpu.VMEM((slots, features), BF16),
+            pltpu.VMEM((slots, features), BF16),
+            pltpu.VMEM((slots // 128, 8, 128), F32),
+            pltpu.VMEM((n, 2, 8, 128), F32),
+            pltpu.VMEM((slots // 128, 8, 128), F32),
+            pltpu.VMEM((n, 2, 8, 128), F32),
+        ] + [pltpu.SemaphoreType.DMA((n,))] * 6 + [
+            pltpu.VMEM((rows, features), F32),
+            pltpu.VMEM((1, rows), jnp.int32),
+            pltpu.VMEM((1, rows), jnp.int32),
+            pltpu.VMEM((1, rows), jnp.int32),
+            pltpu.SemaphoreType.DMA((4,)),
+            pltpu.VMEM((OVER, features), BF16),
+            pltpu.VMEM((OVER, features), BF16),
+            pltpu.VMEM((8, 128), F32),
+            pltpu.VMEM((8, 128), F32),
+            pltpu.VMEM((128, features), BF16),
+            pltpu.VMEM((8, 128), F32),
+            pltpu.VMEM((8, 128), F32),
+            pltpu.SemaphoreType.DMA((2,)),
+            pltpu.SemaphoreType.DMA((2,)),
+            pltpu.SemaphoreType.DMA((n,)),
+            pltpu.SemaphoreType.DMA((n,)),
+            pltpu.SemaphoreType.DMA((2,)),
+        ],
+        compiler_params=pltpu.CompilerParams(
+            collective_id=1, has_side_effects=True, vmem_limit_bytes=32 * 1024 * 1024
+        ),
+        cost_estimate=pl.CostEstimate(
+            flops=2 * slots * features * (rows + slots + CL_DEV),
+            bytes_accessed=4 * rows * features,
+            transcendentals=rows,
+        ),
+    )(
+        embeddings,
+        dest_owner.reshape(1, rows),
+        member_cluster.reshape(1, rows),
+        order.reshape(1, rows),
+    )
+    return lax.cond(
+        flag[0, 0] > 0.5,
+        lambda: fused(embeddings, dest_owner, member_cluster, order, n, cap),
+        lambda: (best.reshape(rows), centroids),
+    )
+
+
 def plain(embeddings, dest_owner, member_cluster, order, owners, capacity):
     rows_here, features = embeddings.shape
     slots = owners * capacity
@@ -290,6 +629,8 @@
     capacity = 2 * embeddings.shape[0] // owners
     blocks_tile = capacity % 16 == 0 and 128 % capacity == 0 and owners & (owners - 1) == 0
     body = fused if blocks_tile else plain
+    if owners == 16 and capacity == 32 and lax.axis_size("groups") == 2:
+        body = relayed
     return body(embeddings, dest_owner, member_cluster, order, owners, capacity)
 
 

time: 42.2 us -> 39.8 us (0.943)
  Pallas kernels: 38.2 us -> 35.9 us
  local copies, waits for them, and re-layouts: 3.13 us -> 2.42 us
  between operations: 0.67 us -> 1.33 us
    pallas_call x1, Pallas kernels: 38.2 us -> 35.9 us  [relayed(): pl.pallas_call(functools.partial(relay_kernel, n, cap), out_shape=(jax.Sh...]
    unnamed x10, local copies, waits for them, and re-layouts: 3.13 us -> 1.91 us
    slice x0 -> x1, local copies, waits for them, and re-layouts: none -> 0.51 us  [relayed(): flag[0, 0] > 0.5]
where the time goes in v3:
time: 39.8 us; the launch traced here: 39.6 us
  Pallas kernels  35.9 us (90%)
  local copies, waits for them, and re-layouts  2.42 us (6%)
  between operations  1.33 us (3%)
    pallas_call x1, Pallas kernels, relayed(): pl.pallas_call(functools.partial(relay_kernel, n, cap), out_shape=(jax.Sh...  35.9 us
    unnamed x10, local copies, waits for them, and re-layouts  1.91 us

profile of v3, /device:TPU:0, one launch (start us, length us, event | category | flops | bytes accessed | tf_op | source)
XLA Modules:
  0.0 39.6 jit_solution(14712731802076792476)
XLA Ops:
  0.6 0.0 copy-start.2
  0.6 0.0 copy-start.3
  0.7 0.0 copy-start.1
  0.7 0.7 %copy-done.2 = s32[256]{0:T(256)S(1)} copy-done((s32[256]{0:T(256)S(1)}, s32[256]{0:T(256)}, u32[]{:S(2)}) %copy-start.2) | copy-done | bytes 1048
  1.3 0.0 copy-done.3
  1.3 0.0 copy-done.1
  1.3 0.0 copy-start
  1.3 35.9 %shard_map.59 = (f32[1,256]{1,0:T(1,128)S(1)}, f32[32,1024]{1,0:T(8,128)S(1)}, f32[8,128]{1,0:T(8,128)S(1)}) custom-call(f32[256,1024]{1,0:T(8,128)} %emb_hbm.1, s32[1,256]{1,0:T(1,128)S(1)} %bitcast.9, s32[1,256]{1,0:T(1,128)S(1)} %bitcast.11, s32[1,256]{1,0:T(1,128)S(1)} %bitcast.13), custom_call_target="tpu_custom_call" | custom-call | flops 838860800 | bytes 1048576 | tf_op jit(solution)/shard_map/pallas_call | solution.py:536
  37.2 0.5 %slice.3 = f32[1,1]{1,0:T(1,128)} slice(f32[8,128]{1,0:T(8,128)S(1)} %get-tuple-element.25), slice={[0:1], [0:1]} | slice | bytes 8 | tf_op jit(solution)/shard_map/slice | solution.py:588
  38.4 0.0 copy-done
  38.4 0.6 %copy.12 = f32[256]{0:T(256)} copy(f32[256]{0:T(256)S(1)} %bitcast.8) | data formatting | bytes 2048
  39.0 0.7 %copy.13 = f32[32,1024]{1,0:T(8,128)} copy(f32[32,1024]{1,0:T(8,128)S(1)} %get-tuple-element.37) | data formatting | bytes 262144
  (1 shorter events, 0.0 us)
Async XLA Ops:
  0.6 0.7 %copy-start.2 = (s32[256]{0:T(256)S(1)}, s32[256]{0:T(256)}, u32[]{:S(2)}) copy-start(s32[256]{0:T(256)} %param.8) | copy-start | bytes 3076
  0.6 0.7 %copy-start.3 = (s32[256]{0:T(256)S(1)}, s32[256]{0:T(256)}, u32[]{:S(2)}) copy-start(s32[256]{0:T(256)} %param.9) | copy-start | bytes 3076
  0.7 0.7 %copy-start.1 = (s32[256]{0:T(256)S(1)}, s32[256]{0:T(256)}, u32[]{:S(2)}) copy-start(s32[256]{0:T(256)} %param.7) | copy-start | bytes 3076
  1.3 37.1 %copy-start = (f32[256,1024]{1,0:T(8,128)S(1)}, f32[256,1024]{1,0:T(8,128)}, u32[]{:S(2)}) copy-start(f32[256,1024]{1,0:T(8,128)} %emb_hbm.1) | copy-start | bytes 3145732

commit v4 on v3

--- a/solution.py
+++ b/solution.py
@@ -153,7 +153,7 @@
     place_copy.start()
     over_copy.start()
     row_copies, key_copies, best_copies, relays = {}, {}, {}, {}
-    for step, t in enumerate((2, 0, 1)):
+    for step, t in enumerate((0, 1, 2)):
         block = jnp.dot(
             pack[t * 128:(t + 1) * 128, :], unit[...], preferred_element_type=F32
         ).astype(BF16)
@@ -279,6 +279,8 @@
         jnp.sum(sums * sums, axis=1, keepdims=True) * (1.0 / features) + EPSILON
     )
 
+    flag_copy.wait()
+    flag_ref[0] = jnp.max(jnp.maximum(flag_out[...], flag_in[...])).astype(jnp.int32)
     for k in range(1, n):
         best_copies[k].wait_recv()
     returned = jnp.concatenate(gathered(best_out, best_in), axis=1)
@@ -291,8 +293,6 @@
     for piece in pieces:
         result = result + jnp.dot(piece, pack[...], preferred_element_type=F32)
     best_ref[...] = result[0:1]
-    flag_copy.wait()
-    flag_ref[...] = jnp.maximum(flag_out[...], flag_in[...])
     over_copy.wait_send()
     place_copy.wait_send()
     for k in range(1, half):
@@ -538,10 +538,10 @@
         out_shape=(
             jax.ShapeDtypeStruct((1, rows), F32),
             jax.ShapeDtypeStruct((CL_DEV, features), F32),
-            jax.ShapeDtypeStruct((8, 128), F32),
+            jax.ShapeDtypeStruct((1,), jnp.int32),
         ),
         in_specs=[pl.BlockSpec(memory_space=pltpu.HBM)] * 4,
-        out_specs=(vmem, vmem, vmem),
+        out_specs=(vmem, vmem, pl.BlockSpec(memory_space=pltpu.SMEM)),
         scratch_shapes=[
             pltpu.VMEM((rows, features), BF16),
             pltpu.VMEM((slots, rows), BF16),
@@ -585,7 +585,7 @@
         order.reshape(1, rows),
     )
     return lax.cond(
-        flag[0, 0] > 0.5,
+        flag[0] > 0,
         lambda: fused(embeddings, dest_owner, member_cluster, order, n, cap),
         lambda: (best.reshape(rows), centroids),
     )

time: 39.8 us -> 38 us (0.955)
  Pallas kernels: 35.9 us -> 34.6 us
  local copies, waits for them, and re-layouts: 2.42 us -> 1.91 us
    pallas_call x1, Pallas kernels: 35.9 us -> 34.6 us  [relayed(): pl.pallas_call(functools.partial(relay_kernel, n, cap), out_shape=(jax.Sh...]
    slice x1 -> x0, local copies, waits for them, and re-layouts: 0.51 us -> none  [relayed(): flag[0, 0] > 0.5]
where the time goes in v4:
time: 38 us; the launch traced here: 37.8 us
  Pallas kernels  34.6 us (91%)
  local copies, waits for them, and re-layouts  1.91 us (5%)
  between operations  1.36 us (4%)
    pallas_call x1, Pallas kernels, relayed(): pl.pallas_call(functools.partial(relay_kernel, n, cap), out_shape=(jax.Sh...  34.6 us
    unnamed x10, local copies, waits for them, and re-layouts  1.91 us

profile of v4, /device:TPU:0, one launch (start us, length us, event | category | flops | bytes accessed | tf_op | source)
XLA Modules:
  0.0 37.8 jit_solution(3632333865185366745)
XLA Ops:
  0.6 0.0 copy-start.2
  0.6 0.0 copy-start.3
  0.7 0.0 copy-start.1
  0.7 0.7 %copy-done.2 = s32[256]{0:T(256)S(1)} copy-done((s32[256]{0:T(256)S(1)}, s32[256]{0:T(256)}, u32[]{:S(2)}) %copy-start.2) | copy-done | bytes 1048
  1.3 0.0 copy-done.3
  1.3 0.0 copy-done.1
  1.3 0.0 copy-start
  1.3 34.6 %shard_map.59 = (f32[1,256]{1,0:T(1,128)S(1)}, f32[32,1024]{1,0:T(8,128)S(1)}, s32[1]{0:T(128)}) custom-call(f32[256,1024]{1,0:T(8,128)} %emb_hbm.1, s32[1,256]{1,0:T(1,128)S(1)} %bitcast.9, s32[1,256]{1,0:T(1,128)S(1)} %bitcast.11, s32[1,256]{1,0:T(1,128)S(1)} %bitcast.13), custom_call_target="tpu_custom_call" | custom-call | flops 838860800 | bytes 1048576 | tf_op jit(solution)/shard_map/pallas_call | solution.py:536
  36.6 0.0 copy-done
  36.6 0.6 %copy.12 = f32[256]{0:T(256)} copy(f32[256]{0:T(256)S(1)} %bitcast.8) | data formatting | bytes 2048
  37.2 0.7 %copy.13 = f32[32,1024]{1,0:T(8,128)} copy(f32[32,1024]{1,0:T(8,128)S(1)} %get-tuple-element.37) | data formatting | bytes 262144
  (1 shorter events, 0.0 us)
Async XLA Ops:
  0.6 0.7 %copy-start.2 = (s32[256]{0:T(256)S(1)}, s32[256]{0:T(256)}, u32[]{:S(2)}) copy-start(s32[256]{0:T(256)} %param.8) | copy-start | bytes 3076
  0.6 0.7 %copy-start.3 = (s32[256]{0:T(256)S(1)}, s32[256]{0:T(256)}, u32[]{:S(2)}) copy-start(s32[256]{0:T(256)} %param.9) | copy-start | bytes 3076
  0.7 0.7 %copy-start.1 = (s32[256]{0:T(256)S(1)}, s32[256]{0:T(256)}, u32[]{:S(2)}) copy-start(s32[256]{0:T(256)} %param.7) | copy-start | bytes 3076
  1.3 35.3 %copy-start = (f32[256,1024]{1,0:T(8,128)S(1)}, f32[256,1024]{1,0:T(8,128)}, u32[]{:S(2)}) copy-start(f32[256,1024]{1,0:T(8,128)} %emb_hbm.1) | copy-start | bytes 3145732
